TPU v7x, 256 devices: a whole 4x4x8 slice. The times are simulated.
256 devices in a mesh: blk: 32 (over z, y_hi, core), grp: 8 (over y_lo, x).
Axes of the slice: x: 4, y: 4 (y_hi: 2, y_lo: 2; y = y_hi * 2 + y_lo), z: 8, core: 2. Of those that a mesh axis runs over, the one named last changes fastest.
Arguments:
- image_vectors: bfloat16 [196608, 1152], P(('blk', 'grp')), may hold values from -12 to 12, as said below
- caption_vectors: bfloat16 [196608, 1152], P(('blk', 'grp')), may hold values from -12 to 12, as said below
- caption_labels: int32 [196608], P(('blk', 'grp')), may hold values from 0 to 196607
- log_logit_scale: float32 [1], replicated, may hold values from 1.6 to 2.4
- logit_offset_bias: float32 [1], replicated, may hold values from -6 to -2
Outputs:
- grad_image: float32 [196608, 1152], P(('blk', 'grp'))
- grad_text: float32 [196608, 1152], P(('blk', 'grp'))
Inputs may be any that keep to these rules, and one draw needn't show every extreme that they name: `image_vectors`: entries of order one. `caption_vectors`: entries of order one.
All inputs are finite; a program needn't handle non-finite values.
Results may differ from a plain program's by a relative error of at most 0.0035.
Values may be sent and summed in bfloat16 or wider, within the bound.
A program may use at most 128 MiB of HBM per device.

v0:
```python
import jax
import jax.numpy as jnp
from jax import lax
from jax.sharding import PartitionSpec as P


def passed_along(value, axis, steps):
    count = lax.axis_size(axis)
    pairs = [(source, (source + steps) % count) for source in range(count)]
    return lax.ppermute(value, axis, pairs)


def from_partner(shard, axis, stride):
    return lax.ppermute(shard, axis, [(i, i ^ 1 << stride) for i in range(lax.axis_size(axis))])


def normalize(embedding):
    values = embedding.astype(jnp.float32)
    inverse = lax.rsqrt(jnp.sum(values * values, axis=-1, keepdims=True) + 1e-06)
    return (values * inverse, inverse)


def pairwise_weight(image_lower, text_lower, image_labels, text_labels, logit_scale, shifted_bias):
    similarity_products = lax.dot_general(
        image_lower, text_lower, (((1,), (1,)), ((), ())), preferred_element_type=jnp.float32
    )
    pair_logits = logit_scale * similarity_products + shifted_bias
    positive_mask = (image_labels[:, None] == text_labels[None, :]).astype(jnp.float32)
    return ((jax.nn.sigmoid(pair_logits) - positive_mask) * logit_scale).astype(jnp.bfloat16)


def image_side(weight_tile_matrix, text_lower):
    return jnp.dot(weight_tile_matrix, text_lower, preferred_element_type=jnp.float32)


def text_side(weight_tile_matrix, image_lower):
    return lax.dot_general(
        weight_tile_matrix,
        image_lower,
        (((0,), (0,)), ((), ())),
        preferred_element_type=jnp.float32,
    )


def project_back(direction, inverse, gradient):
    return inverse * (gradient - direction * jnp.sum(direction * gradient, axis=-1, keepdims=True))


def local(image_vectors, caption_vectors, caption_labels, log_logit_scale, logit_offset_bias):
    logit_scale = jnp.exp(log_logit_scale[0])
    shifted_bias = logit_offset_bias[0]
    image_dir, image_inv = normalize(image_vectors)
    text_dir, text_inv = normalize(caption_vectors)
    image_lower = image_dir.astype(jnp.bfloat16)
    text_lower = text_dir.astype(jnp.bfloat16)
    text_neighbour, neighbour_labels = passed_along((text_lower, caption_labels), "blk", 1)
    text_companion, companion_labels = from_partner((text_lower, caption_labels), "grp", 0)
    local_tile = pairwise_weight(
        image_lower, text_lower, caption_labels, caption_labels, logit_scale, shifted_bias
    )
    grad_image_dir = image_side(local_tile, text_lower)
    grad_text_dir = text_side(local_tile, image_lower)
    left_tile = pairwise_weight(
        image_lower, text_neighbour, caption_labels, neighbour_labels, logit_scale, shifted_bias
    )
    grad_image_dir = grad_image_dir + image_side(left_tile, text_neighbour)
    returned = passed_along(text_side(left_tile, image_lower), "blk", -1)
    grad_text_dir = grad_text_dir + returned
    partner_tile = pairwise_weight(
        image_lower, text_companion, caption_labels, companion_labels, logit_scale, shifted_bias
    )
    grad_image_dir = grad_image_dir + image_side(partner_tile, text_companion)
    returned_partner = from_partner(
        text_side(partner_tile, image_lower).astype(jnp.bfloat16), "grp", 0
    ).astype(jnp.float32)
    grad_text_dir = grad_text_dir + returned_partner
    grad_image = project_back(image_dir, image_inv, grad_image_dir)
    grad_text = project_back(text_dir, text_inv, grad_text_dir)
    return (grad_image, grad_text)


def solution(mesh):
    in_specs = (P(("blk", "grp"), None), P(("blk", "grp"), None), P(("blk", "grp")), P(), P())
    out_specs = (P(("blk", "grp"), None), P(("blk", "grp"), None))
    return jax.shard_map(local, mesh=mesh, in_specs=in_specs, out_specs=out_specs, check_vma=False)
```

profile of v0, /device:TPU:1, one launch (start us, length us, event | category | flops | bytes accessed | tf_op | source)
XLA Modules:
  0.0 96.7 jit_solution(7842925573308593655)
XLA Ops:
  0.6 0.0 copy-start.1
  0.6 0.0 copy-start.2
  0.6 0.0 copy-start
  0.7 2.0 %fusion.14 = f32[768]{0:T(1024)S(1)} fusion(bf16[768,1152]{1,0:T(8,128)(2,1)} %param.6), kind=kLoop, calls=%fused_computation.21 | loop fusion | flops 2653440 | bytes 1772544 | tf_op jit(solution)/shard_map/reduce_sum | solution.py:19
  2.7 0.0 copy-done.1
  2.7 0.4 fusion.2
  3.1 4.4 %collective-permute-start = (bf16[768,1152]{1,0:T(8,128)(2,1)S(1)}, bf16[768,1152]{1,0:T(8,128)(2,1)S(1)}, u32[]{:S(2)}, u32[]{:S(2)}) collective-permute-start(bf16[768,1152]{1,0:T(8,128)(2,1)S(1)} %fusion.2), channel_id=1, source_target_pairs={{0,8},{8,16},{16,24},{24,32},{32,40},{40,48},{48,56},{56,64},{64,7... | collective-permute-start | bytes 5308424 | tf_op jit(solution)/shard_map/ppermute | solution.py:10
  7.5 1.2 %collective-permute-start.2 = (bf16[768,1152]{1,0:T(8,128)(2,1)S(1)}, bf16[768,1152]{1,0:T(8,128)(2,1)S(1)}, u32[]{:S(2)}, u32[]{:S(2)}) collective-permute-start(bf16[768,1152]{1,0:T(8,128)(2,1)S(1)} %fusion.2), channel_id=1, source_target_pairs={{0,1},{1,0},{2,3},{3,2},{4,5},{5,4},{6,7},{7,6},{8,9},{9,8},{10,11... | collective-permute-start | bytes 5308424 | tf_op jit(solution)/shard_map/ppermute | solution.py:14
  8.7 0.0 copy-done.2
  8.7 0.4 collective-permute-start.1
  9.1 0.3 collective-permute-start.3
  9.3 0.0 copy-done
  9.3 0.4 fusion.10
  11.1 15.9 %collective-permute-done.1 = s32[768]{0:T(1024)S(1)} collective-permute-done((s32[768]{0:T(1024)S(1)}, s32[768]{0:T(1024)S(1)}, u32[]{:S(2)}, u32[]{:S(2)}) %collective-permute-start.1) | collective-permute-done | bytes 3104 | tf_op jit(solution)/shard_map/ppermute | solution.py:10
  27.0 0.0 collective-permute-done
  27.0 2.4 %multiply_convert_fusion.1 = bf16[768,768]{1,0:T(8,128)(2,1)S(1)} fusion(bf16[768,1152]{1,0:T(8,128)(2,1)S(1)} %collective-permute-done, s32[768]{0:T(1024)S(1)} %collective-permute-done.1, f32[]{:T(128)} %bitcast.16, f32[]{:T(128)} %bitcast, s32[768]{0:T(1024)S(1)} %copy-done.2, bf16[768,1152]{1,0:T(8,128)(2,1)S(1)} %copy-done, f32[768]{0:T(1024)S(1)} %add_rsqrt_fusion.1), kind=kOutput, calls=%fused_computation.24 | convolution fusion | flops 1367506944 | bytes 4727816 | tf_op jit(solution)/shard_map/dot_general | solution.py:24
  29.4 1.8 %fusion.16 = f32[768,1152]{1,0:T(8,128)S(1)} fusion(bf16[768,768]{1,0:T(8,128)(2,1)S(1)} %multiply_convert_fusion.1, bf16[768,1152]{1,0:T(8,128)(2,1)S(1)} %copy-done, f32[768]{0:T(1024)S(1)} %add_rsqrt_fusion.1), kind=kOutput, calls=%fused_computation.28 | convolution fusion | flops 1361608704 | bytes 6491136 | tf_op jit(solution)/shard_map/dot_general | solution.py:37
  31.2 6.1 %collective-permute-start.4 = (f32[768,1152]{1,0:T(8,128)S(1)}, f32[768,1152]{1,0:T(8,128)S(1)}, u32[]{:S(2)}, u32[]{:S(2)}) collective-permute-start(f32[768,1152]{1,0:T(8,128)S(1)} %fusion.16), channel_id=1, source_target_pairs={{0,248},{8,0},{16,8},{24,16},{32,24},{40,32},{48,40},{56,48},{64,5... | collective-permute-start | bytes 10616840 | tf_op jit(solution)/shard_map/ppermute | solution.py:10
  37.4 2.4 %multiply_convert_fusion.2 = bf16[768,768]{1,0:T(8,128)(2,1)S(1)} fusion(bf16[768,1152]{1,0:T(8,128)(2,1)S(1)} %fusion.2, s32[768]{0:T(1024)S(1)} %copy-done.2, f32[]{:T(128)} %bitcast.14, f32[]{:T(128)} %bitcast, bf16[768,1152]{1,0:T(8,128)(2,1)S(1)} %copy-done, f32[768]{0:T(1024)S(1)} %add_rsqrt_fusion.1), kind=kOutput, calls=%fused_computation.25 | convolution fusion | flops 1367506944 | bytes 4724744 | tf_op jit(solution)/shard_map/dot_general | solution.py:24
  39.8 1.7 %fusion.22 = f32[768,1152]{1,0:T(8,128)S(1)} fusion(bf16[768,768]{1,0:T(8,128)(2,1)S(1)} %multiply_convert_fusion.2, bf16[768,1152]{1,0:T(8,128)(2,1)S(1)} %fusion.2), kind=kOutput, calls=%fused_computation.29 | convolution fusion | flops 1358954496 | bytes 6488064 | tf_op jit(solution)/shard_map/dot_general | solution.py:33
  41.5 5.9 %collective-permute-done.3 = s32[768]{0:T(1024)S(1)} collective-permute-done((s32[768]{0:T(1024)S(1)}, s32[768]{0:T(1024)S(1)}, u32[]{:S(2)}, u32[]{:S(2)}) %collective-permute-start.3) | collective-permute-done | bytes 3104 | tf_op jit(solution)/shard_map/ppermute | solution.py:14
  47.4 0.0 collective-permute-done.2
  47.4 2.4 %multiply_convert_fusion = bf16[768,768]{1,0:T(8,128)(2,1)S(1)} fusion(bf16[768,1152]{1,0:T(8,128)(2,1)S(1)} %collective-permute-done.2, s32[768]{0:T(1024)S(1)} %collective-permute-done.3, f32[]{:T(128)} %bitcast.15, f32[]{:T(128)} %bitcast, s32[768]{0:T(1024)S(1)} %copy-done.2, bf16[768,1152]{1,0:T(8,128)(2,1)S(1)} %copy-done, f32[768]{0:T(1024)S(1)} %add_rsqrt_fusion.1), kind=kOutput, calls=%fused_computation.23 | convolution fusion | flops 1367506944 | bytes 4727816 | tf_op jit(solution)/shard_map/dot_general | solution.py:24
  49.8 1.8 %convolution_convert_fusion = bf16[768,1152]{1,0:T(8,128)(2,1)S(1)} fusion(bf16[768,768]{1,0:T(8,128)(2,1)S(1)} %multiply_convert_fusion, bf16[768,1152]{1,0:T(8,128)(2,1)S(1)} %copy-done, f32[768]{0:T(1024)S(1)} %add_rsqrt_fusion.1), kind=kOutput, calls=%fused_computation.22 | convolution fusion | flops 1362493440 | bytes 4721664 | tf_op jit(solution)/shard_map/dot_general | solution.py:37
  51.7 0.3 collective-permute-start.5
  52.0 1.7 %convolution_add_fusion.2 = f32[768,1152]{1,0:T(8,128)S(1)} fusion(f32[768,1152]{1,0:T(8,128)S(1)} %fusion.22, bf16[768,768]{1,0:T(8,128)(2,1)S(1)} %multiply_convert_fusion.1, bf16[768,1152]{1,0:T(8,128)(2,1)S(1)} %collective-permute-done), kind=kOutput, calls=%fused_computation.13 | convolution fusion | flops 1359839232 | bytes 10027008 | tf_op jit(solution)/shard_map/dot_general | solution.py:33
  53.7 2.0 %fusion.7 = (f32[768]{0:T(1024)S(1)}, f32[768,1152]{1,0:T(8,128)S(1)}) fusion(bf16[768,1152]{1,0:T(8,128)(2,1)S(1)} %copy-done, f32[768]{0:T(1024)S(1)} %add_rsqrt_fusion.1, f32[768,1152]{1,0:T(8,128)S(1)} %convolution_add_fusion.2, bf16[768,768]{1,0:T(8,128)(2,1)S(1)} %multiply_convert_fusion, bf16[768,1152]{1,0:T(8,128)(2,1)S(1)} %collective-permute-done.2), kind=kOutput, calls=%fused_computation.14 | convolution fusion | flops 1363377408 | bytes 11802624 | tf_op jit(solution)/shard_map/dot_general | solution.py:33
  55.7 2.5 %fusion.9 = f32[768,1152]{1,0:T(8,128)} fusion(f32[768,1152]{1,0:T(8,128)S(1)} %get-tuple-element.3, bf16[768,1152]{1,0:T(8,128)(2,1)S(1)} %copy-done, f32[768]{0:T(1024)S(1)} %get-tuple-element.2, f32[768]{0:T(1024)S(1)} %add_rsqrt_fusion.1), kind=kLoop, calls=%fused_computation.16 | loop fusion | flops 4423680 | bytes 8853504 | tf_op jit(solution)/shard_map/mul | solution.py:46
  58.1 33.9 %collective-permute-done.5 = bf16[768,1152]{1,0:T(8,128)(2,1)S(1)} collective-permute-done((bf16[768,1152]{1,0:T(8,128)(2,1)S(1)}, bf16[768,1152]{1,0:T(8,128)(2,1)S(1)}, u32[]{:S(2)}, u32[]{:S(2)}) %collective-permute-start.5) | collective-permute-done | bytes 1769504 | tf_op jit(solution)/shard_map/ppermute | solution.py:14
  92.0 0.0 collective-permute-done.4
  92.0 2.2 %fusion.11 = (f32[768]{0:T(1024)S(1)}, f32[768,1152]{1,0:T(8,128)S(1)}) fusion(bf16[768,1152]{1,0:T(8,128)(2,1)S(1)} %copy-done.1, f32[768]{0:T(1024)S(1)} %add_rsqrt_fusion, bf16[768,1152]{1,0:T(8,128)(2,1)S(1)} %collective-permute-done.5, f32[768,1152]{1,0:T(8,128)S(1)} %collective-permute-done.4, bf16[768,768]{1,0:T(8,128)(2,1)S(1)} %multiply_convert_fusion.2, ...), kind=kOutput, calls=%fused_computation.18 | convolution fusion | flops 1367801088 | bytes 13575168 | tf_op jit(solution)/shard_map/dot_general | solution.py:37
  94.2 2.5 %fusion.13 = f32[768,1152]{1,0:T(8,128)} fusion(f32[768,1152]{1,0:T(8,128)S(1)} %get-tuple-element.5, bf16[768,1152]{1,0:T(8,128)(2,1)S(1)} %copy-done.1, f32[768]{0:T(1024)S(1)} %get-tuple-element.4, f32[768]{0:T(1024)S(1)} %add_rsqrt_fusion), kind=kLoop, calls=%fused_computation.20 | loop fusion | flops 4423680 | bytes 8853504 | tf_op jit(solution)/shard_map/mul | solution.py:46
  (2 shorter events, 0.0 us)
Async XLA Ops:
  0.6 2.1 %copy-start.1 = (bf16[768,1152]{1,0:T(8,128)(2,1)S(1)}, bf16[768,1152]{1,0:T(8,128)(2,1)}, u32[]{:S(2)}) copy-start(bf16[768,1152]{1,0:T(8,128)(2,1)} %param.6) | copy-start | bytes 5308420
  0.6 8.0 %copy-start.2 = (s32[768]{0:T(1024)S(1)}, s32[768]{0:T(1024)}, u32[]{:S(2)}) copy-start(s32[768]{0:T(1024)} %param.7) | copy-start | bytes 9220
  0.6 8.7 %copy-start = (bf16[768,1152]{1,0:T(8,128)(2,1)S(1)}, bf16[768,1152]{1,0:T(8,128)(2,1)}, u32[]{:S(2)}) copy-start(bf16[768,1152]{1,0:T(8,128)(2,1)} %param.5) | copy-start | bytes 5308420
  3.1 23.9 %collective-permute-start = (bf16[768,1152]{1,0:T(8,128)(2,1)S(1)}, bf16[768,1152]{1,0:T(8,128)(2,1)S(1)}, u32[]{:S(2)}, u32[]{:S(2)}) collective-permute-start(bf16[768,1152]{1,0:T(8,128)(2,1)S(1)} %fusion.2), channel_id=1, source_target_pairs={{0,8},{8,16},{16,24},{24,32},{32,40},{40,48},{48,56},{56,64},{64,7... | collective-permute-start | bytes 5308424 | tf_op jit(solution)/shard_map/ppermute | solution.py:10
  7.5 39.9 %collective-permute-start.2 = (bf16[768,1152]{1,0:T(8,128)(2,1)S(1)}, bf16[768,1152]{1,0:T(8,128)(2,1)S(1)}, u32[]{:S(2)}, u32[]{:S(2)}) collective-permute-start(bf16[768,1152]{1,0:T(8,128)(2,1)S(1)} %fusion.2), channel_id=1, source_target_pairs={{0,1},{1,0},{2,3},{3,2},{4,5},{5,4},{6,7},{7,6},{8,9},{9,8},{10,11... | collective-permute-start | bytes 5308424 | tf_op jit(solution)/shard_map/ppermute | solution.py:14
  8.7 18.3 %collective-permute-start.1 = (s32[768]{0:T(1024)S(1)}, s32[768]{0:T(1024)S(1)}, u32[]{:S(2)}, u32[]{:S(2)}) collective-permute-start(s32[768]{0:T(1024)S(1)} %copy-done.2), channel_id=1, source_target_pairs={{0,8},{8,16},{16,24},{24,32},{32,40},{40,48},{48,56},{56,64},{64,7... | collective-permute-start | bytes 9224 | tf_op jit(solution)/shard_map/ppermute | solution.py:10
  9.1 38.3 %collective-permute-start.3 = (s32[768]{0:T(1024)S(1)}, s32[768]{0:T(1024)S(1)}, u32[]{:S(2)}, u32[]{:S(2)}) collective-permute-start(s32[768]{0:T(1024)S(1)} %copy-done.2), channel_id=1, source_target_pairs={{0,1},{1,0},{2,3},{3,2},{4,5},{5,4},{6,7},{7,6},{8,9},{9,8},{10,11... | collective-permute-start | bytes 9224 | tf_op jit(solution)/shard_map/ppermute | solution.py:14
  31.2 60.7 %collective-permute-start.4 = (f32[768,1152]{1,0:T(8,128)S(1)}, f32[768,1152]{1,0:T(8,128)S(1)}, u32[]{:S(2)}, u32[]{:S(2)}) collective-permute-start(f32[768,1152]{1,0:T(8,128)S(1)} %fusion.16), channel_id=1, source_target_pairs={{0,248},{8,0},{16,8},{24,16},{32,24},{40,32},{48,40},{56,48},{64,5... | collective-permute-start | bytes 10616840 | tf_op jit(solution)/shard_map/ppermute | solution.py:10
  51.7 40.3 %collective-permute-start.5 = (bf16[768,1152]{1,0:T(8,128)(2,1)S(1)}, bf16[768,1152]{1,0:T(8,128)(2,1)S(1)}, u32[]{:S(2)}, u32[]{:S(2)}) collective-permute-start(bf16[768,1152]{1,0:T(8,128)(2,1)S(1)} %convolution_convert_fusion), channel_id=1, source_target_pairs={{0,1},{1,0},{2,3},{3,2},{4,5},{5,4},{6,7},{7,6},{8,9},{9,8},{10,11... | collective-permute-start | bytes 5308424 | tf_op jit(solution)/shard_map/ppermute | solution.py:14
where the time goes:
time: 96.8 us; the launch traced here: 96.7 us
  waiting for transfers between devices  55.7 us (58%)
  matrix products  18.5 us (19%)
  starting transfers between devices  12.7 us (13%)
  other arithmetic  7.74 us (8%)
  between operations  2.09 us (2%)
    ppermute x3, waiting for transfers between devices, from_partner(): lax.ppermute(shard, axis, [(i, i ^ 1 << stride) for i in range(lax.axis_s...  39.8 us
    ppermute x3, waiting for transfers between devices, passed_along(): return lax.ppermute(value, axis, pairs)  15.9 us
    ppermute x3, starting transfers between devices, passed_along(): return lax.ppermute(value, axis, pairs)  10.9 us
    dot_general x3, matrix products, pairwise_weight(): lax.dot_general(image_lower, text_lower, (((1,), (1,)), ((), ())), prefer...  7.23 us
    dot_general x3, matrix products, text_side(): lax.dot_general(weight_tile_matrix, image_lower, (((0,), (0,)), ((), ()))...  5.93 us
    dot_general x3, matrix products, image_side(): jnp.dot(weight_tile_matrix, text_lower, preferred_element_type=jnp.float32)  5.37 us
    mul x2, other arithmetic, project_back(): inverse * (gradient - direction * jnp.sum(direction * gradient, axis=-1,...  4.92 us
    reduce_sum x2, other arithmetic, normalize(): jnp.sum(values * values, axis=-1, keepdims=True) + 1e-06  2.45 us
  transfers between devices with their start and end apart: 6, of which 3 were waited for; matrix products, arithmetic and copies ran while one was open for 20% of the time, Pallas kernels for 0%

commit v1 on v0

v1 whole, which is shorter than its diff:
```python
import jax
import jax.numpy as jnp
from jax import lax
from jax.experimental import pallas as pl
from jax.experimental.pallas import tpu as pltpu
from jax.sharding import PartitionSpec as P

ROWS = 768
WIDTH = 1152
STEP = 256
STEPS = ROWS // STEP
PIECE = 128
PIECES = ROWS // PIECE
LANES = 128
MESH = pl.DeviceIdType.MESH


def rows_of(index, size):
    return pl.ds(pl.multiple_of(index * size, size), size)


def normalize_rows(source, rows, low, low_rows, inverse=None):
    values = source[rows, :].astype(jnp.float32)
    scaled = lax.rsqrt(jnp.sum(values * values, axis=-1, keepdims=True) + 1e-06)
    low[low_rows, :] = (values * scaled).astype(jnp.bfloat16)
    if inverse is not None:
        inverse[rows, :] = scaled


def kernel(
    image_hbm,
    caption_hbm,
    labels_hbm,
    log_scale,
    offset,
    grad_image,
    grad_text,
    image,
    caption,
    labels,
    image_low,
    text_low,
    image_inv,
    text_inv,
    label_column,
    left_labels,
    partner_labels,
    left_text,
    partner_text,
    low,
    part,
    left_out,
    partner_out,
    left_in,
    partner_in,
    local_sems,
    label_send,
    label_recv,
    left_send,
    left_recv,
    partner_send,
    partner_recv,
    left_back_send,
    left_back_recv,
    partner_back_send,
    partner_back_recv,
):
    blk, grp = lax.axis_index("blk"), lax.axis_index("grp")
    count = lax.axis_size("blk")
    right = (lax.rem(blk + 1, count), grp)
    left = (lax.rem(blk + count - 1, count), grp)
    partner = (blk, grp + 1 - 2 * lax.rem(grp, 2))

    loads = [
        pltpu.make_async_copy(source, target, local_sems.at[i])
        for i, (source, target) in enumerate(((labels_hbm, labels), (image_hbm, image), (caption_hbm, caption)))
    ]
    for load in loads:
        load.start()

    barrier = pltpu.get_barrier_semaphore()
    for other in (partner, right, left):
        pl.semaphore_signal(barrier, inc=1, device_id=other, device_id_type=MESH)
    pl.semaphore_wait(barrier, 3)

    def remote(source, target, send, recv, device):
        return pltpu.make_async_remote_copy(source, target, send, recv, device_id=device, device_id_type=MESH)

    def text_copy(target, send, recv, device, i):
        rows = rows_of(i, STEP)
        return remote(caption_hbm.at[rows, :], target.at[rows, :], send.at[i], recv.at[i], device)

    to_partner = [text_copy(partner_text, partner_send, partner_recv, partner, i) for i in range(STEPS)]
    to_right = [text_copy(left_text, left_send, left_recv, right, i) for i in range(STEPS)]
    label_copies = [
        remote(labels_hbm, partner_labels, label_send.at[0], label_recv.at[0], partner),
        remote(labels_hbm, left_labels, label_send.at[1], label_recv.at[1], right),
    ]
    for copy in label_copies:
        copy.start()
    for a, b in zip(to_partner, to_right):
        a.start()
        b.start()

    def left_back(i):
        rows = rows_of(i, STEP)
        return remote(left_out.at[rows, :], left_in.at[rows, :], left_back_send.at[i], left_back_recv.at[i], left)

    def partner_back(i):
        rows = rows_of(i, PIECE)
        return remote(
            partner_out.at[rows, :], partner_in.at[rows, :], partner_back_send.at[i], partner_back_recv.at[i], partner
        )

    scale = jnp.exp(jnp.full((1, STEP), log_scale[0], jnp.float32))
    bias = offset[0]

    loads[0].wait()
    for i in range(ROWS // LANES):
        label_column[i * LANES : (i + 1) * LANES, :] = jnp.broadcast_to(labels[i : i + 1, :], (LANES, LANES)).T

    loads[1].wait()

    @pl.loop(0, PIECES)
    def _(i):
        rows = rows_of(i, PIECE)
        normalize_rows(image, rows, image_low, rows, image_inv)

    loads[2].wait()

    @pl.loop(0, PIECES)
    def _(i):
        rows = rows_of(i, PIECE)
        normalize_rows(caption, rows, text_low, rows, text_inv)

    def tile(step, text, text_rows, text_labels, first):
        per = STEP // LANES
        row = jnp.concatenate([text_labels[pl.ds(step * per + j, 1), :] for j in range(per)], axis=1)

        @pl.loop(0, ROWS // STEP)
        def _(m):
            rows = rows_of(m, STEP)
            images = image_low[rows, :]
            texts = text[text_rows, :]
            products = lax.dot_general(images, texts, (((1,), (1,)), ((), ())), preferred_element_type=jnp.float32)
            column = jnp.concatenate([label_column[rows, :]] * per, axis=1)
            positive = (column == row).astype(jnp.float32)
            weight = ((jax.nn.sigmoid(scale * products + bias) - positive) * scale).astype(jnp.bfloat16)
            update = jnp.dot(weight, texts, preferred_element_type=jnp.float32)

            @pl.when(jnp.logical_and(first, step == 0))
            def _():
                grad_image[rows, :] = update

            @pl.when(jnp.logical_not(jnp.logical_and(first, step == 0)))
            def _():
                grad_image[rows, :] += update

            back = lax.dot_general(weight, images, (((0,), (0,)), ((), ())), preferred_element_type=jnp.float32)

            @pl.when(m == 0)
            def _():
                part[...] = back

            @pl.when(m > 0)
            def _():
                part[...] += back

    @pl.loop(0, STEPS)
    def _(c):
        rows = rows_of(c, STEP)
        tile(c, text_low, rows, labels, True)
        grad_text[rows, :] = part[...]

    def normalize_arrived(text, c):
        @pl.loop(0, STEP // PIECE)
        def _(i):
            normalize_rows(text, rows_of(c * (STEP // PIECE) + i, PIECE), low, rows_of(i, PIECE))

    label_copies[1].wait()

    @pl.loop(0, STEPS)
    def _(c):
        text_copy(left_text, left_send, left_recv, right, c).wait_recv()
        normalize_arrived(left_text, c)
        tile(c, low, pl.ds(0, STEP), left_labels, False)
        left_out[rows_of(c, STEP), :] = part[...].astype(jnp.bfloat16)
        left_back(c).start()

    label_copies[0].wait()

    @pl.loop(0, STEPS)
    def _(c):
        text_copy(partner_text, partner_send, partner_recv, partner, c).wait_recv()
        normalize_arrived(partner_text, c)
        tile(c, low, pl.ds(0, STEP), partner_labels, False)
        partner_out[rows_of(c, STEP), :] = part[...].astype(jnp.bfloat16)
        for j in range(STEP // PIECE):
            partner_back(c * (STEP // PIECE) + j).start()

    def project_back(grad, source, inverse, rows, gradient):
        inv = inverse[rows, :]
        direction = source[rows, :].astype(jnp.float32) * inv
        along = jnp.sum(direction * gradient, axis=-1, keepdims=True)
        grad[rows, :] = inv * (gradient - direction * along)

    @pl.loop(0, PIECES)
    def _(i):
        rows = rows_of(i, PIECE)
        project_back(grad_image, image, image_inv, rows, grad_image[rows, :])

    @pl.loop(0, STEPS)
    def _(c):
        left_back(c).wait_recv()
        rows = rows_of(c, STEP)
        grad_text[rows, :] += left_in[rows, :].astype(jnp.float32)

    for c in range(STEPS):
        to_right[c].wait_send()
        to_partner[c].wait_send()
        left_back(c).wait_send()

    @pl.loop(0, PIECES)
    def _(i):
        partner_back(i).wait()
        rows = rows_of(i, PIECE)
        gradient = grad_text[rows, :] + partner_in[rows, :].astype(jnp.float32)
        project_back(grad_text, caption, text_inv, rows, gradient)


def local(image_vectors, caption_vectors, caption_labels, log_logit_scale, logit_offset_bias):
    block = (ROWS, WIDTH)
    label_block = (ROWS // LANES, LANES)
    hbm = pl.BlockSpec(memory_space=pltpu.HBM)
    smem = pl.BlockSpec(memory_space=pltpu.SMEM)
    vmem = pl.BlockSpec(memory_space=pltpu.VMEM)
    dma = pltpu.SemaphoreType.DMA
    low_block = pltpu.VMEM(block, jnp.bfloat16)
    return pl.pallas_call(
        kernel,
        out_shape=(pltpu.VMEM(block, jnp.float32), pltpu.VMEM(block, jnp.float32)),
        in_specs=[hbm, hbm, hbm, smem, smem],
        out_specs=(vmem, vmem),
        scratch_shapes=[
            low_block,
            low_block,
            pltpu.VMEM(label_block, jnp.int32),
            low_block,
            low_block,
            pltpu.VMEM((ROWS, 1), jnp.float32),
            pltpu.VMEM((ROWS, 1), jnp.float32),
            pltpu.VMEM((ROWS, LANES), jnp.int32),
            pltpu.VMEM(label_block, jnp.int32),
            pltpu.VMEM(label_block, jnp.int32),
            low_block,
            low_block,
            pltpu.VMEM((STEP, WIDTH), jnp.bfloat16),
            pltpu.VMEM((STEP, WIDTH), jnp.float32),
            low_block,
            low_block,
            low_block,
            low_block,
            dma((3,)),
            dma((2,)),
            dma((2,)),
            dma((STEPS,)),
            dma((STEPS,)),
            dma((STEPS,)),
            dma((STEPS,)),
            dma((STEPS,)),
            dma((STEPS,)),
            dma((PIECES,)),
            dma((PIECES,)),
        ],
        compiler_params=pltpu.CompilerParams(
            collective_id=0, has_side_effects=True, vmem_limit_bytes=32 * 1024 * 1024
        ),
        cost_estimate=pl.CostEstimate(
            flops=18 * ROWS * ROWS * WIDTH, bytes_accessed=12 * ROWS * WIDTH, transcendentals=3 * ROWS * ROWS
        ),
        name="contrast",
    )(
        pltpu.with_memory_space_constraint(image_vectors, pltpu.HBM),
        pltpu.with_memory_space_constraint(caption_vectors, pltpu.HBM),
        pltpu.with_memory_space_constraint(caption_labels.reshape(label_block), pltpu.HBM),
        log_logit_scale,
        logit_offset_bias,
    )


def solution(mesh):
    rows = P(("blk", "grp"), None)
    return jax.shard_map(
        local, mesh=mesh, in_specs=(rows, rows, P(("blk", "grp")), P(), P()), out_specs=(rows, rows), check_vma=False
    )
```

time: 96.8 us -> 88.1 us (0.910)
  the two profiles are of different devices: /device:TPU:1 before, /device:TPU:164 now
where the time goes in v1:
time: 88.1 us; the launch traced here: 87.7 us
  Pallas kernels  82.2 us (93%)
  local copies, waits for them, and re-layouts  3.59 us (4%)
  between operations  1.93 us (2%)
    pallas_call x1, Pallas kernels, local(): pl.pallas_call(kernel, out_shape=(pltpu.VMEM(block, jnp.float32), pltpu.V...  82.2 us
    unnamed x2, local copies, waits for them, and re-layouts  3.59 us

profile of v1, /device:TPU:164, one launch (start us, length us, event | category | flops | bytes accessed | tf_op | source)
XLA Modules:
  0.0 87.7 jit_solution(15007319044668593740)
XLA Ops:
  1.9 82.2 %contrast.1 = (f32[768,1152]{1,0:T(8,128)S(1)}, f32[768,1152]{1,0:T(8,128)S(1)}) custom-call(bf16[768,1152]{1,0:T(8,128)(2,1)} %image_hbm.1, bf16[768,1152]{1,0:T(8,128)(2,1)} %caption_hbm.1, s32[6,128]{1,0:T(8,128)} %bitcast.1, f32[1]{0:T(128)S(6)} %copy.11.log_scale, f32[1]{0:T(128)S(6)} %copy.12.offset), custom_call_target="tpu_custom_call" | custom-call | flops 12230590464 | bytes 10616832 | tf_op jit(solution)/shard_map/contrast/pallas_call | solution.py:239
  84.1 1.8 %copy.9 = f32[768,1152]{1,0:T(8,128)} copy(f32[768,1152]{1,0:T(8,128)S(1)} %get-tuple-element.2) | data formatting | bytes 7077888
  85.9 1.8 %copy.10 = f32[768,1152]{1,0:T(8,128)} copy(f32[768,1152]{1,0:T(8,128)S(1)} %get-tuple-element.3) | data formatting | bytes 7077888

commit v2 on v1

--- a/solution.py
+++ b/solution.py
@@ -12,6 +12,7 @@
 PIECE = 128
 PIECES = ROWS // PIECE
 LANES = 128
+WRITES = 1
 MESH = pl.DeviceIdType.MESH
 
 
@@ -54,6 +55,7 @@
     left_in,
     partner_in,
     local_sems,
+    inside_sem,
     label_send,
     label_recv,
     left_send,
@@ -71,6 +73,41 @@
     left = (lax.rem(blk + count - 1, count), grp)
     partner = (blk, grp + 1 - 2 * lax.rem(grp, 2))
 
+    first_core = lax.rem(blk, 2) == 0
+
+    barrier = pltpu.get_barrier_semaphore()
+    pl.semaphore_signal(barrier, inc=1, device_id=partner, device_id_type=MESH)
+
+    @pl.when(jnp.logical_not(first_core))
+    def _():
+        pl.semaphore_signal(barrier, inc=1, device_id=right, device_id_type=MESH)
+        pl.semaphore_signal(barrier, inc=1, device_id=left, device_id_type=MESH)
+
+    @pl.when(first_core)
+    def _():
+        pl.semaphore_wait(barrier, 3)
+
+    @pl.when(jnp.logical_not(first_core))
+    def _():
+        pl.semaphore_wait(barrier, 1)
+
+    def remote(source, target, send, recv, device):
+        return pltpu.make_async_remote_copy(source, target, send, recv, device_id=device, device_id_type=MESH)
+
+    def text_copy(target, send, recv, device, i):
+        rows = rows_of(i, STEP)
+        return remote(caption_hbm.at[rows, :], target.at[rows, :], send.at[i], recv.at[i], device)
+
+    to_partner = [text_copy(partner_text, partner_send, partner_recv, partner, i) for i in range(STEPS)]
+    to_right = [text_copy(left_text, left_send, left_recv, right, i) for i in range(STEPS)]
+    label_copies = [
+        remote(labels_hbm, partner_labels, label_send.at[0], label_recv.at[0], partner),
+        remote(labels_hbm, left_labels, label_send.at[1], label_recv.at[1], right),
+    ]
+    label_copies[0].start()
+    for copy in to_partner:
+        copy.start()
+
     loads = [
         pltpu.make_async_copy(source, target, local_sems.at[i])
         for i, (source, target) in enumerate(((labels_hbm, labels), (image_hbm, image), (caption_hbm, caption)))
@@ -78,29 +115,9 @@
     for load in loads:
         load.start()
 
-    barrier = pltpu.get_barrier_semaphore()
-    for other in (partner, right, left):
-        pl.semaphore_signal(barrier, inc=1, device_id=other, device_id_type=MESH)
-    pl.semaphore_wait(barrier, 3)
-
-    def remote(source, target, send, recv, device):
-        return pltpu.make_async_remote_copy(source, target, send, recv, device_id=device, device_id_type=MESH)
-
-    def text_copy(target, send, recv, device, i):
-        rows = rows_of(i, STEP)
-        return remote(caption_hbm.at[rows, :], target.at[rows, :], send.at[i], recv.at[i], device)
-
-    to_partner = [text_copy(partner_text, partner_send, partner_recv, partner, i) for i in range(STEPS)]
-    to_right = [text_copy(left_text, left_send, left_recv, right, i) for i in range(STEPS)]
-    label_copies = [
-        remote(labels_hbm, partner_labels, label_send.at[0], label_recv.at[0], partner),
-        remote(labels_hbm, left_labels, label_send.at[1], label_recv.at[1], right),
-    ]
-    for copy in label_copies:
-        copy.start()
-    for a, b in zip(to_partner, to_right):
-        a.start()
-        b.start()
+    @pl.when(first_core)
+    def _():
+        pl.semaphore_signal(inside_sem, inc=1, device_id=left, device_id_type=MESH)
 
     def left_back(i):
         rows = rows_of(i, STEP)
@@ -125,6 +142,14 @@
     def _(i):
         rows = rows_of(i, PIECE)
         normalize_rows(image, rows, image_low, rows, image_inv)
+
+    @pl.when(jnp.logical_not(first_core))
+    def _():
+        pl.semaphore_wait(inside_sem, 1)
+
+    label_copies[1].start()
+    for copy in to_right:
+        copy.start()
 
     loads[2].wait()
 
@@ -228,6 +253,18 @@
         project_back(grad_text, caption, text_inv, rows, gradient)
 
 
+def write_out(grad_image, grad_text, image_out, text_out, sems):
+    copies = [
+        pltpu.make_async_copy(source.at[rows_of(i, ROWS // WRITES), :], target.at[rows_of(i, ROWS // WRITES), :], sems.at[j, i])
+        for i in range(WRITES)
+        for j, (source, target) in enumerate(((grad_image, image_out), (grad_text, text_out)))
+    ]
+    for copy in copies:
+        copy.start()
+    for copy in copies:
+        copy.wait()
+
+
 def local(image_vectors, caption_vectors, caption_labels, log_logit_scale, logit_offset_bias):
     block = (ROWS, WIDTH)
     label_block = (ROWS // LANES, LANES)
@@ -236,7 +273,7 @@
     vmem = pl.BlockSpec(memory_space=pltpu.VMEM)
     dma = pltpu.SemaphoreType.DMA
     low_block = pltpu.VMEM(block, jnp.bfloat16)
-    return pl.pallas_call(
+    grads = pl.pallas_call(
         kernel,
         out_shape=(pltpu.VMEM(block, jnp.float32), pltpu.VMEM(block, jnp.float32)),
         in_specs=[hbm, hbm, hbm, smem, smem],
@@ -261,6 +298,7 @@
             low_block,
             low_block,
             dma((3,)),
+            pltpu.SemaphoreType.REGULAR,
             dma((2,)),
             dma((2,)),
             dma((STEPS,)),
@@ -280,12 +318,27 @@
         ),
         name="contrast",
     )(
-        pltpu.with_memory_space_constraint(image_vectors, pltpu.HBM),
-        pltpu.with_memory_space_constraint(caption_vectors, pltpu.HBM),
-        pltpu.with_memory_space_constraint(caption_labels.reshape(label_block), pltpu.HBM),
+        *(
+            pltpu.with_memory_space_constraint(value, pltpu.HBM)
+            for value in (
+                image_vectors,
+                caption_vectors,
+                caption_labels.reshape(label_block),
+            )
+        ),
         log_logit_scale,
         logit_offset_bias,
     )
+    return pl.pallas_call(
+        write_out,
+        out_shape=(jax.ShapeDtypeStruct(block, jnp.float32),) * 2,
+        in_specs=[vmem] * 2,
+        out_specs=(pl.BlockSpec(memory_space=pl.ANY),) * 2,
+        scratch_shapes=[dma((2, WRITES))],
+        compiler_params=pltpu.CompilerParams(vmem_limit_bytes=16 * 1024 * 1024),
+        cost_estimate=pl.CostEstimate(flops=0, bytes_accessed=16 * ROWS * WIDTH, transcendentals=0),
+        name="write_out",
+    )(*(pltpu.with_memory_space_constraint(value, pltpu.VMEM) for value in grads))
 
 
 def solution(mesh):

time: 88.1 us -> 84.3 us (0.957)
  local copies, waits for them, and re-layouts: 3.59 us -> 0 us
    unnamed x2 -> x0, local copies, waits for them, and re-layouts: 3.59 us -> none
    pallas_call x0 -> x1, Pallas kernels: none -> 2.98 us  [local(): pl.pallas_call(write_out, out_shape=(jax.ShapeDtypeStruct(block, jnp.floa...]
    pallas_call x1, Pallas kernels: 82.2 us -> 79.3 us  [local(): pl.pallas_call(kernel, out_shape=(pltpu.VMEM(block, jnp.float32), pltpu.V...]
where the time goes in v2:
time: 84.3 us; the launch traced here: 84.2 us
  Pallas kernels  82.3 us (98%)
  between operations  1.93 us (2%)
    pallas_call x1, Pallas kernels, local(): pl.pallas_call(kernel, out_shape=(pltpu.VMEM(block, jnp.float32), pltpu.V...  79.3 us
    pallas_call x1, Pallas kernels, local(): pl.pallas_call(write_out, out_shape=(jax.ShapeDtypeStruct(block, jnp.floa...  2.98 us

profile of v2, /device:TPU:164, one launch (start us, length us, event | category | flops | bytes accessed | tf_op | source)
XLA Modules:
  0.0 84.2 jit_solution(14466926266536522637)
XLA Ops:
  1.9 79.3 %contrast.1 = (f32[768,1152]{1,0:T(8,128)S(1)}, f32[768,1152]{1,0:T(8,128)S(1)}) custom-call(bf16[768,1152]{1,0:T(8,128)(2,1)} %image_hbm.1, bf16[768,1152]{1,0:T(8,128)(2,1)} %caption_hbm.1, s32[6,128]{1,0:T(8,128)} %bitcast.1, f32[1]{0:T(128)S(6)} %copy.7.log_scale, f32[1]{0:T(128)S(6)} %copy.8.offset), custom_call_target="tpu_custom_call" | custom-call | flops 12230590464 | bytes 10616832 | tf_op jit(solution)/shard_map/contrast/pallas_call | solution.py:276
  81.2 3.0 %write_out.1 = (f32[768,1152]{1,0:T(8,128)}, f32[768,1152]{1,0:T(8,128)}) custom-call(f32[768,1152]{1,0:T(8,128)S(1)} %get-tuple-element.4.grad_image, f32[768,1152]{1,0:T(8,128)S(1)} %get-tuple-element.5.grad_text), custom_call_target="tpu_custom_call" | custom-call | bytes 14155776 | tf_op jit(solution)/shard_map/write_out/pallas_call | solution.py:332

commit v3 on v2

--- a/solution.py
+++ b/solution.py
@@ -12,7 +12,8 @@
 PIECE = 128
 PIECES = ROWS // PIECE
 LANES = 128
-WRITES = 1
+EARLY = 2
+ENDS = tuple((i * PIECE, PIECE) for i in range(EARLY, PIECES - 1)) + ((640, 64), (704, 64))
 MESH = pl.DeviceIdType.MESH
 
 
@@ -36,6 +37,7 @@
     offset,
     grad_image,
     grad_text,
+    partner_out,
     image,
     caption,
     labels,
@@ -51,7 +53,6 @@
     low,
     part,
     left_out,
-    partner_out,
     left_in,
     partner_in,
     local_sems,
@@ -104,6 +105,16 @@
         remote(labels_hbm, partner_labels, label_send.at[0], label_recv.at[0], partner),
         remote(labels_hbm, left_labels, label_send.at[1], label_recv.at[1], right),
     ]
+    def send_right():
+        label_copies[1].start()
+        for copy in to_right:
+            copy.start()
+
+    @pl.when(first_core)
+    def _():
+        pl.semaphore_signal(inside_sem, inc=1, device_id=left, device_id_type=MESH)
+        send_right()
+
     label_copies[0].start()
     for copy in to_partner:
         copy.start()
@@ -115,10 +126,6 @@
     for load in loads:
         load.start()
 
-    @pl.when(first_core)
-    def _():
-        pl.semaphore_signal(inside_sem, inc=1, device_id=left, device_id_type=MESH)
-
     def left_back(i):
         rows = rows_of(i, STEP)
         return remote(left_out.at[rows, :], left_in.at[rows, :], left_back_send.at[i], left_back_recv.at[i], left)
@@ -146,10 +153,7 @@
     @pl.when(jnp.logical_not(first_core))
     def _():
         pl.semaphore_wait(inside_sem, 1)
-
-    label_copies[1].start()
-    for copy in to_right:
-        copy.start()
+        send_right()
 
     loads[2].wait()
 
@@ -220,19 +224,18 @@
         normalize_arrived(partner_text, c)
         tile(c, low, pl.ds(0, STEP), partner_labels, False)
         partner_out[rows_of(c, STEP), :] = part[...].astype(jnp.bfloat16)
+
         for j in range(STEP // PIECE):
-            partner_back(c * (STEP // PIECE) + j).start()
-
-    def project_back(grad, source, inverse, rows, gradient):
-        inv = inverse[rows, :]
-        direction = source[rows, :].astype(jnp.float32) * inv
-        along = jnp.sum(direction * gradient, axis=-1, keepdims=True)
-        grad[rows, :] = inv * (gradient - direction * along)
+            piece = c * (STEP // PIECE) + j
+
+            @pl.when(jnp.logical_or(first_core, piece < EARLY))
+            def _():
+                partner_back(piece).start()
 
     @pl.loop(0, PIECES)
     def _(i):
         rows = rows_of(i, PIECE)
-        project_back(grad_image, image, image_inv, rows, grad_image[rows, :])
+        grad_image[rows, :] = project_back(image[rows, :], image_inv[rows, :], grad_image[rows, :])
 
     @pl.loop(0, STEPS)
     def _(c):
@@ -245,24 +248,91 @@
         to_partner[c].wait_send()
         left_back(c).wait_send()
 
-    @pl.loop(0, PIECES)
+    @pl.loop(0, jnp.where(first_core, PIECES, EARLY))
     def _(i):
         partner_back(i).wait()
         rows = rows_of(i, PIECE)
         gradient = grad_text[rows, :] + partner_in[rows, :].astype(jnp.float32)
-        project_back(grad_text, caption, text_inv, rows, gradient)
-
-
-def write_out(grad_image, grad_text, image_out, text_out, sems):
-    copies = [
-        pltpu.make_async_copy(source.at[rows_of(i, ROWS // WRITES), :], target.at[rows_of(i, ROWS // WRITES), :], sems.at[j, i])
-        for i in range(WRITES)
-        for j, (source, target) in enumerate(((grad_image, image_out), (grad_text, text_out)))
-    ]
-    for copy in copies:
-        copy.start()
-    for copy in copies:
-        copy.wait()
+        grad_text[rows, :] = project_back(caption[rows, :], text_inv[rows, :], gradient)
+
+
+def project_back(source, inv, gradient):
+    direction = source.astype(jnp.float32) * inv
+    along = jnp.sum(direction * gradient, axis=-1, keepdims=True)
+    return inv * (gradient - direction * along)
+
+
+def finish(caption_hbm, grad_in, partner_out, image_out, grad_text, caption, partner_in, load_sem, send, recv):
+    blk, grp = lax.axis_index("blk"), lax.axis_index("grp")
+    partner = (blk, grp + 1 - 2 * lax.rem(grp, 2))
+    first_core = lax.rem(blk, 2) == 0
+    barrier = pltpu.get_barrier_semaphore()
+    load = pltpu.make_async_copy(caption_hbm, caption, load_sem)
+
+    @pl.when(jnp.logical_not(first_core))
+    def _():
+        pl.semaphore_signal(barrier, inc=1, device_id=partner, device_id_type=MESH)
+        load.start()
+        pl.semaphore_wait(barrier, 1)
+
+    def back(i):
+        rows = pl.ds(*ENDS[i])
+        return pltpu.make_async_remote_copy(
+            partner_out.at[rows, :],
+            partner_in.at[rows, :],
+            send.at[i],
+            recv.at[i],
+            device_id=partner,
+            device_id_type=MESH,
+        )
+
+    def rows_back(rows, source):
+        values = caption[rows, :].astype(jnp.float32)
+        inv = lax.rsqrt(jnp.sum(values * values, axis=-1, keepdims=True) + 1e-06)
+        gradient = grad_in[rows, :] + source[rows, :].astype(jnp.float32)
+        grad_text[rows, :] = project_back(caption[rows, :], inv, gradient)
+
+    def done_rows(pieces):
+        @pl.loop(0, pieces)
+        def _(i):
+            rows = rows_of(i, PIECE)
+            grad_text[rows, :] = grad_in[rows, :]
+
+    @pl.when(jnp.logical_not(first_core))
+    def _():
+        copies = [back(i) for i in range(len(ENDS))]
+        for copy in copies:
+            copy.start()
+        done_rows(EARLY)
+        load.wait()
+        for copy, end in zip(copies, ENDS):
+            copy.wait_recv()
+            rows_back(pl.ds(*end), partner_in)
+        for copy in copies:
+            copy.wait_send()
+
+    @pl.when(first_core)
+    def _():
+        done_rows(PIECES)
+
+
+def write_out(source, target, sem):
+    copy = pltpu.make_async_copy(source, target, sem)
+    copy.start()
+    copy.wait()
+
+
+def written(value):
+    return pl.pallas_call(
+        write_out,
+        out_shape=jax.ShapeDtypeStruct(value.shape, value.dtype),
+        in_specs=[pl.BlockSpec(memory_space=pltpu.VMEM)],
+        out_specs=pl.BlockSpec(memory_space=pl.ANY),
+        scratch_shapes=[pltpu.SemaphoreType.DMA(())],
+        compiler_params=pltpu.CompilerParams(vmem_limit_bytes=4 * 1024 * 1024),
+        cost_estimate=pl.CostEstimate(flops=0, bytes_accessed=8 * ROWS * WIDTH, transcendentals=0),
+        name="write_out",
+    )(pltpu.with_memory_space_constraint(value, pltpu.VMEM))
 
 
 def local(image_vectors, caption_vectors, caption_labels, log_logit_scale, logit_offset_bias):
@@ -273,11 +343,12 @@
     vmem = pl.BlockSpec(memory_space=pltpu.VMEM)
     dma = pltpu.SemaphoreType.DMA
     low_block = pltpu.VMEM(block, jnp.bfloat16)
-    grads = pl.pallas_call(
+    captions = pltpu.with_memory_space_constraint(caption_vectors, pltpu.HBM)
+    grad_image, grad_text, partner_out = pl.pallas_call(
         kernel,
-        out_shape=(pltpu.VMEM(block, jnp.float32), pltpu.VMEM(block, jnp.float32)),
+        out_shape=(pltpu.VMEM(block, jnp.float32),) * 2 + (low_block,),
         in_specs=[hbm, hbm, hbm, smem, smem],
-        out_specs=(vmem, vmem),
+        out_specs=(vmem,) * 3,
         scratch_shapes=[
             low_block,
             low_block,
@@ -293,7 +364,6 @@
             low_block,
             pltpu.VMEM((STEP, WIDTH), jnp.bfloat16),
             pltpu.VMEM((STEP, WIDTH), jnp.float32),
-            low_block,
             low_block,
             low_block,
             low_block,
@@ -329,16 +399,20 @@
         log_logit_scale,
         logit_offset_bias,
     )
-    return pl.pallas_call(
-        write_out,
-        out_shape=(jax.ShapeDtypeStruct(block, jnp.float32),) * 2,
-        in_specs=[vmem] * 2,
-        out_specs=(pl.BlockSpec(memory_space=pl.ANY),) * 2,
-        scratch_shapes=[dma((2, WRITES))],
-        compiler_params=pltpu.CompilerParams(vmem_limit_bytes=16 * 1024 * 1024),
-        cost_estimate=pl.CostEstimate(flops=0, bytes_accessed=16 * ROWS * WIDTH, transcendentals=0),
-        name="write_out",
-    )(*(pltpu.with_memory_space_constraint(value, pltpu.VMEM) for value in grads))
+    image_out = written(grad_image)
+    grad_text = pl.pallas_call(
+        finish,
+        out_shape=pltpu.VMEM(block, jnp.float32),
+        in_specs=[hbm, vmem, vmem, hbm],
+        out_specs=vmem,
+        scratch_shapes=[low_block, low_block, dma(()), dma((len(ENDS),)), dma((len(ENDS),))],
+        compiler_params=pltpu.CompilerParams(
+            collective_id=1, has_side_effects=True, vmem_limit_bytes=16 * 1024 * 1024
+        ),
+        cost_estimate=pl.CostEstimate(flops=ROWS * WIDTH, bytes_accessed=8 * ROWS * WIDTH, transcendentals=0),
+        name="finish",
+    )(captions, *(pltpu.with_memory_space_constraint(v, pltpu.VMEM) for v in (grad_text, partner_out)), pltpu.with_memory_space_constraint(image_out, pltpu.HBM))
+    return image_out, written(grad_text)
 
 
 def solution(mesh):

time: 84.3 us -> 83.6 us (level)
    pallas_call x2 -> x4, Pallas kernels: 82.3 us -> 81.5 us  [the longest x1 77.4 us: local(): pl.pallas_call(kernel, out_shape=(pltpu.VMEM(block, jnp.float32),) * 2 +...]
where the time goes in v3:
time: 83.6 us; the launch traced here: 83.5 us
  Pallas kernels  81.5 us (97%)
  between operations  1.95 us (2%)
    pallas_call x1, Pallas kernels, local(): pl.pallas_call(kernel, out_shape=(pltpu.VMEM(block, jnp.float32),) * 2 +...  77.4 us
    pallas_call x2, Pallas kernels, written(): pl.pallas_call(write_out, out_shape=jax.ShapeDtypeStruct(value.shape, val...  3.61 us

profile of v3, /device:TPU:164, one launch (start us, length us, event | category | flops | bytes accessed | tf_op | source)
XLA Modules:
  0.0 83.5 jit_solution(14188536532539714362)
XLA Ops:
  1.9 77.4 %contrast.1 = (f32[768,1152]{1,0:T(8,128)S(1)}, f32[768,1152]{1,0:T(8,128)S(1)}, bf16[768,1152]{1,0:T(8,128)(2,1)S(1)}) custom-call(bf16[768,1152]{1,0:T(8,128)(2,1)} %image_hbm.1, bf16[768,1152]{1,0:T(8,128)(2,1)} %caption_hbm.3, s32[6,128]{1,0:T(8,128)} %bitcast.1, f32[1]{0:T(128)S(6)} %copy.7.log_scale, f32[1]{0:T(128)S(6)} %copy.8.offset), custom_call_target="tpu_custom_call" | custom-call | flops 12230590464 | bytes 10616832 | tf_op jit(solution)/shard_map/contrast/pallas_call | solution.py:347
  79.3 1.8 %write_out.2.image_out = f32[768,1152]{1,0:T(8,128)} custom-call(f32[768,1152]{1,0:T(8,128)S(1)} %get-tuple-element.5.source), custom_call_target="tpu_custom_call" | custom-call | bytes 7077888 | tf_op jit(solution)/shard_map/write_out/pallas_call | solution.py:326
  81.1 0.5 finish.1.source
  81.7 1.8 %write_out.3 = f32[768,1152]{1,0:T(8,128)} custom-call(f32[768,1152]{1,0:T(8,128)S(1)} %finish.1.source), custom_call_target="tpu_custom_call" | custom-call | bytes 7077888 | tf_op jit(solution)/shard_map/write_out/pallas_call | solution.py:326

commit v4 on v3

--- a/solution.py
+++ b/solution.py
@@ -286,53 +286,52 @@
             device_id_type=MESH,
         )
 
-    def rows_back(rows, source):
+    def rows_back(start, size, source):
+        rows = pl.ds(start, size)
         values = caption[rows, :].astype(jnp.float32)
         inv = lax.rsqrt(jnp.sum(values * values, axis=-1, keepdims=True) + 1e-06)
         gradient = grad_in[rows, :] + source[rows, :].astype(jnp.float32)
-        grad_text[rows, :] = project_back(caption[rows, :], inv, gradient)
-
-    def done_rows(pieces):
-        @pl.loop(0, pieces)
+        grad_text[pl.ds(start - EARLY * PIECE, size), :] = project_back(caption[rows, :], inv, gradient)
+
+    def done_rows():
+        @pl.loop(EARLY, PIECES)
         def _(i):
             rows = rows_of(i, PIECE)
-            grad_text[rows, :] = grad_in[rows, :]
+            grad_text[rows_of(i - EARLY, PIECE), :] = grad_in[rows, :]
 
     @pl.when(jnp.logical_not(first_core))
     def _():
         copies = [back(i) for i in range(len(ENDS))]
         for copy in copies:
             copy.start()
-        done_rows(EARLY)
         load.wait()
         for copy, end in zip(copies, ENDS):
             copy.wait_recv()
-            rows_back(pl.ds(*end), partner_in)
+            rows_back(*end, partner_in)
         for copy in copies:
             copy.wait_send()
 
     @pl.when(first_core)
     def _():
-        done_rows(PIECES)
-
-
-def write_out(source, target, sem):
-    copy = pltpu.make_async_copy(source, target, sem)
+        done_rows()
+
+
+def write_early(grad_image, grad_text, image_out, text_out, sems):
+    rows = pl.ds(0, EARLY * PIECE)
+    copies = [
+        pltpu.make_async_copy(grad_image, image_out, sems.at[0]),
+        pltpu.make_async_copy(grad_text.at[rows, :], text_out.at[rows, :], sems.at[1]),
+    ]
+    for copy in copies:
+        copy.start()
+    for copy in copies:
+        copy.wait()
+
+
+def write_late(late, text_in, text_out, sem):
+    copy = pltpu.make_async_copy(late, text_out.at[pl.ds(EARLY * PIECE, ROWS - EARLY * PIECE), :], sem)
     copy.start()
     copy.wait()
-
-
-def written(value):
-    return pl.pallas_call(
-        write_out,
-        out_shape=jax.ShapeDtypeStruct(value.shape, value.dtype),
-        in_specs=[pl.BlockSpec(memory_space=pltpu.VMEM)],
-        out_specs=pl.BlockSpec(memory_space=pl.ANY),
-        scratch_shapes=[pltpu.SemaphoreType.DMA(())],
-        compiler_params=pltpu.CompilerParams(vmem_limit_bytes=4 * 1024 * 1024),
-        cost_estimate=pl.CostEstimate(flops=0, bytes_accessed=8 * ROWS * WIDTH, transcendentals=0),
-        name="write_out",
-    )(pltpu.with_memory_space_constraint(value, pltpu.VMEM))
 
 
 def local(image_vectors, caption_vectors, caption_labels, log_logit_scale, logit_offset_bias):
@@ -399,10 +398,21 @@
         log_logit_scale,
         logit_offset_bias,
     )
-    image_out = written(grad_image)
-    grad_text = pl.pallas_call(
+    any_space = pl.BlockSpec(memory_space=pl.ANY)
+    whole = jax.ShapeDtypeStruct(block, jnp.float32)
+    image_out, text_out = pl.pallas_call(
+        write_early,
+        out_shape=(whole, whole),
+        in_specs=[vmem, vmem],
+        out_specs=(any_space, any_space),
+        scratch_shapes=[dma((2,))],
+        compiler_params=pltpu.CompilerParams(vmem_limit_bytes=4 * 1024 * 1024),
+        cost_estimate=pl.CostEstimate(flops=0, bytes_accessed=8 * ROWS * WIDTH, transcendentals=0),
+        name="write_early",
+    )(*(pltpu.with_memory_space_constraint(v, pltpu.VMEM) for v in (grad_image, grad_text)))
+    late = pl.pallas_call(
         finish,
-        out_shape=pltpu.VMEM(block, jnp.float32),
+        out_shape=pltpu.VMEM((ROWS - EARLY * PIECE, WIDTH), jnp.float32),
         in_specs=[hbm, vmem, vmem, hbm],
         out_specs=vmem,
         scratch_shapes=[low_block, low_block, dma(()), dma((len(ENDS),)), dma((len(ENDS),))],
@@ -411,8 +421,23 @@
         ),
         cost_estimate=pl.CostEstimate(flops=ROWS * WIDTH, bytes_accessed=8 * ROWS * WIDTH, transcendentals=0),
         name="finish",
-    )(captions, *(pltpu.with_memory_space_constraint(v, pltpu.VMEM) for v in (grad_text, partner_out)), pltpu.with_memory_space_constraint(image_out, pltpu.HBM))
-    return image_out, written(grad_text)
+    )(
+        captions,
+        *(pltpu.with_memory_space_constraint(v, pltpu.VMEM) for v in (grad_text, partner_out)),
+        pltpu.with_memory_space_constraint(image_out, pltpu.HBM),
+    )
+    text_out = pl.pallas_call(
+        write_late,
+        out_shape=whole,
+        in_specs=[vmem, any_space],
+        out_specs=any_space,
+        scratch_shapes=[dma(())],
+        input_output_aliases={1: 0},
+        compiler_params=pltpu.CompilerParams(vmem_limit_bytes=4 * 1024 * 1024),
+        cost_estimate=pl.CostEstimate(flops=0, bytes_accessed=8 * ROWS * WIDTH, transcendentals=0),
+        name="write_late",
+    )(pltpu.with_memory_space_constraint(late, pltpu.VMEM), text_out)
+    return image_out, text_out
 
 
 def solution(mesh):

time: 83.6 us -> 83.1 us (level)
  no operation moved by 1% of the time
where the time goes in v4:
time: 83.1 us; the launch traced here: 83 us
  Pallas kernels  81.1 us (98%)
  between operations  1.95 us (2%)
    pallas_call x1, Pallas kernels, local(): pl.pallas_call(kernel, out_shape=(pltpu.VMEM(block, jnp.float32),) * 2 +...  77 us
    pallas_call x1, Pallas kernels, local(): pl.pallas_call(write_early, out_shape=(whole, whole), in_specs=[vmem, vme...  2.2 us

profile of v4, /device:TPU:164, one launch (start us, length us, event | category | flops | bytes accessed | tf_op | source)
XLA Modules:
  0.0 83.0 jit_solution(12910901742036888085)
XLA Ops:
  1.9 77.0 %contrast.1 = (f32[768,1152]{1,0:T(8,128)S(1)}, f32[768,1152]{1,0:T(8,128)S(1)}, bf16[768,1152]{1,0:T(8,128)(2,1)S(1)}) custom-call(bf16[768,1152]{1,0:T(8,128)(2,1)} %image_hbm.1, bf16[768,1152]{1,0:T(8,128)(2,1)} %caption_hbm.3, s32[6,128]{1,0:T(8,128)} %bitcast.1, f32[1]{0:T(128)S(6)} %copy.9.log_scale, f32[1]{0:T(128)S(6)} %copy.10.offset), custom_call_target="tpu_custom_call" | custom-call | flops 12230590464 | bytes 10616832 | tf_op jit(solution)/shard_map/contrast/pallas_call | solution.py:346
  78.9 2.2 %write_early.1 = (f32[768,1152]{1,0:T(8,128)}, f32[768,1152]{1,0:T(8,128)}) custom-call(f32[768,1152]{1,0:T(8,128)S(1)} %get-tuple-element.7.grad_image, f32[768,1152]{1,0:T(8,128)S(1)} %get-tuple-element.8.grad_text.grad_in), custom_call_target="tpu_custom_call" | custom-call | bytes 7077888 | tf_op jit(solution)/shard_map/write_early/pallas_call | solution.py:403
  81.1 0.4 finish.1.late
  81.6 1.4 %write_late.1 = f32[768,1152]{1,0:T(8,128)} custom-call(f32[512,1152]{1,0:T(8,128)S(1)} %finish.1.late, f32[768,1152]{1,0:T(8,128)} %get-tuple-element.11.text_in), custom_call_target="tpu_custom_call", output_to_operand_aliasing={{}: (1, {})} | custom-call | bytes 7077888 | tf_op jit(solution)/shard_map/write_late/pallas_call | solution.py:429

commit v5 on v4

--- a/solution.py
+++ b/solution.py
@@ -293,12 +293,6 @@
         gradient = grad_in[rows, :] + source[rows, :].astype(jnp.float32)
         grad_text[pl.ds(start - EARLY * PIECE, size), :] = project_back(caption[rows, :], inv, gradient)
 
-    def done_rows():
-        @pl.loop(EARLY, PIECES)
-        def _(i):
-            rows = rows_of(i, PIECE)
-            grad_text[rows_of(i - EARLY, PIECE), :] = grad_in[rows, :]
-
     @pl.when(jnp.logical_not(first_core))
     def _():
         copies = [back(i) for i in range(len(ENDS))]
@@ -311,27 +305,32 @@
         for copy in copies:
             copy.wait_send()
 
-    @pl.when(first_core)
-    def _():
-        done_rows()
-
 
 def write_early(grad_image, grad_text, image_out, text_out, sems):
-    rows = pl.ds(0, EARLY * PIECE)
+    early, late = pl.ds(0, EARLY * PIECE), pl.ds(EARLY * PIECE, ROWS - EARLY * PIECE)
     copies = [
         pltpu.make_async_copy(grad_image, image_out, sems.at[0]),
-        pltpu.make_async_copy(grad_text.at[rows, :], text_out.at[rows, :], sems.at[1]),
+        pltpu.make_async_copy(grad_text.at[early, :], text_out.at[early, :], sems.at[1]),
     ]
     for copy in copies:
         copy.start()
+
+    @pl.when(lax.rem(lax.axis_index("blk"), 2) == 0)
+    def _():
+        rest = pltpu.make_async_copy(grad_text.at[late, :], text_out.at[late, :], sems.at[2])
+        rest.start()
+        rest.wait()
+
     for copy in copies:
         copy.wait()
 
 
 def write_late(late, text_in, text_out, sem):
-    copy = pltpu.make_async_copy(late, text_out.at[pl.ds(EARLY * PIECE, ROWS - EARLY * PIECE), :], sem)
-    copy.start()
-    copy.wait()
+    @pl.when(lax.rem(lax.axis_index("blk"), 2) == 1)
+    def _():
+        copy = pltpu.make_async_copy(late, text_out.at[pl.ds(EARLY * PIECE, ROWS - EARLY * PIECE), :], sem)
+        copy.start()
+        copy.wait()
 
 
 def local(image_vectors, caption_vectors, caption_labels, log_logit_scale, logit_offset_bias):
@@ -405,7 +404,7 @@
         out_shape=(whole, whole),
         in_specs=[vmem, vmem],
         out_specs=(any_space, any_space),
-        scratch_shapes=[dma((2,))],
+        scratch_shapes=[dma((3,))],
         compiler_params=pltpu.CompilerParams(vmem_limit_bytes=4 * 1024 * 1024),
         cost_estimate=pl.CostEstimate(flops=0, bytes_accessed=8 * ROWS * WIDTH, transcendentals=0),
         name="write_early",

time: 83.1 us -> 83.1 us (level)
    pallas_call x1, Pallas kernels: 1.42 us -> 0.03 us  [local(): pl.pallas_call(write_late, out_shape=whole, in_specs=[vmem, any_space], o...]
where the time goes in v5:
time: 83.1 us; the launch traced here: 82.2 us
  Pallas kernels  80.3 us (97%)
  between operations  1.95 us (2%)
    pallas_call x1, Pallas kernels, local(): pl.pallas_call(kernel, out_shape=(pltpu.VMEM(block, jnp.float32),) * 2 +...  77 us
    pallas_call x1, Pallas kernels, local(): pl.pallas_call(write_early, out_shape=(whole, whole), in_specs=[vmem, vme...  2.99 us

profile of v5, /device:TPU:164, one launch (start us, length us, event | category | flops | bytes accessed | tf_op | source)
XLA Modules:
  0.0 82.2 jit_solution(13883649979297531130)
XLA Ops:
  1.9 77.0 %contrast.1 = (f32[768,1152]{1,0:T(8,128)S(1)}, f32[768,1152]{1,0:T(8,128)S(1)}, bf16[768,1152]{1,0:T(8,128)(2,1)S(1)}) custom-call(bf16[768,1152]{1,0:T(8,128)(2,1)} %image_hbm.1, bf16[768,1152]{1,0:T(8,128)(2,1)} %caption_hbm.3, s32[6,128]{1,0:T(8,128)} %bitcast.1, f32[1]{0:T(128)S(6)} %copy.9.log_scale, f32[1]{0:T(128)S(6)} %copy.10.offset), custom_call_target="tpu_custom_call" | custom-call | flops 12230590464 | bytes 10616832 | tf_op jit(solution)/shard_map/contrast/pallas_call | solution.py:345
  78.9 3.0 %write_early.1 = (f32[768,1152]{1,0:T(8,128)}, f32[768,1152]{1,0:T(8,128)}) custom-call(f32[768,1152]{1,0:T(8,128)S(1)} %get-tuple-element.7.grad_image, f32[768,1152]{1,0:T(8,128)S(1)} %get-tuple-element.8.grad_text.grad_in), custom_call_target="tpu_custom_call" | custom-call | bytes 7077888 | tf_op jit(solution)/shard_map/write_early/pallas_call | solution.py:402
  81.9 0.3 finish.1.late
  (1 shorter events, 0.0 us)
